TPU v7x, 32 devices: a whole 2x2x4 slice. The times are simulated.
32 devices in a mesh: dp: 16 (over z, y, x), mp: 2 (over core).
Axes of the slice: x: 2, y: 2, z: 4, core: 2. Of those that a mesh axis runs over, the one named last changes fastest.
Arguments:
- short_input: bfloat16 [64, 128, 768], P('dp'), may hold values from -6 to 6
- long_input: bfloat16 [16, 512, 768], P('dp'), may hold values from -6 to 6
- query_weight: bfloat16 [768, 768], P(None, 'mp'), may hold values from -0.21875 to 0.21875
- query_bias: bfloat16 [768], P('mp'), may hold values from -3 to 3
- key_weight: bfloat16 [768, 768], P(None, 'mp'), may hold values from -0.21875 to 0.21875
- value_weight: bfloat16 [768, 768], P(None, 'mp'), may hold values from -0.21875 to 0.21875
- value_bias: bfloat16 [768], P('mp'), may hold values from -3 to 3
- output_weight: bfloat16 [768, 768], P('mp'), may hold values from -0.875 to 0.875
- output_bias: bfloat16 [768], replicated, may hold values from -3 to 3
- gain_one: bfloat16 [768], replicated, may hold values from 0.25 to 1.75
- shift_one: bfloat16 [768], replicated, may hold values from -2 to 2
- upward_weight: bfloat16 [768, 3072], P(None, 'mp'), may hold values from -0.21875 to 0.21875
- upward_bias: bfloat16 [3072], P('mp'), may hold values from -3 to 3
- downward_weight: bfloat16 [3072, 768], P('mp'), may hold values from -0.109375 to 0.109375
- downward_bias: bfloat16 [768], replicated, may hold values from -3 to 3
- gain_two: bfloat16 [768], replicated, may hold values from 0.25 to 1.75
- shift_two: bfloat16 [768], replicated, may hold values from -2 to 2
- short_upstream: bfloat16 [64, 128, 768], P('dp'), may hold values from -6 to 6
- long_upstream: bfloat16 [16, 512, 768], P('dp'), may hold values from -6 to 6
- short_lengths: int32 [64], P('dp'), may hold values from 64 to 128, as said below
- long_lengths: int32 [16], P('dp'), may hold values from 256 to 512, as said below
- live_counts: int32 [16, 2], P('dp'), may hold values from 0 to 4, as said below
Outputs:
- short_output: bfloat16 [64, 128, 768], P('dp')
- long_output: bfloat16 [16, 512, 768], P('dp')
- short_inputgrad: bfloat16 [64, 128, 768], P('dp')
- long_inputgrad: bfloat16 [16, 512, 768], P('dp')
- query_grad: float32 [768, 768], P('dp', 'mp')
- querybias_grad: float32 [768], P(('mp', 'dp'))
- key_grad: float32 [768, 768], P('dp', 'mp')
- value_grad: float32 [768, 768], P('dp', 'mp')
- valuebias_grad: float32 [768], P(('mp', 'dp'))
- output_grad: float32 [768, 768], P('mp', 'dp')
- outbias_grad: float32 [768], P('dp')
- gainone_grad: float32 [768], P('dp')
- shiftone_grad: float32 [768], P('dp')
- upward_grad: float32 [768, 3072], P('dp', 'mp')
- upbias_grad: float32 [3072], P(('mp', 'dp'))
- downward_grad: float32 [3072, 768], P('mp', 'dp')
- downbias_grad: float32 [768], P('dp')
- gaintwo_grad: float32 [768], P('dp')
- shifttwo_grad: float32 [768], P('dp')
Inputs may be any that keep to these rules, and one draw needn't show every extreme that they name: `short_lengths`: in every draw some short slot holds 128 tokens and some holds 64. `long_lengths`: in every draw some long slot holds 512 tokens and some holds 256. `live_counts`: column 0 counts a device's live short slots, 2 to 4; column 1 its live long slots, 0 or 1; the live slots are a device's first ones; in every draw some device has all slots live and another has the fewest of both kinds.
All inputs are finite; a program needn't handle non-finite values.
Results may differ from a plain program's by a relative error of at most 0.02.
Values may be sent and summed in bfloat16 or wider, within the bound.
A program may use at most 128 MiB of HBM per device.

v0:
```python
import jax
import jax.numpy as jnp
from jax import lax
from jax.sharding import PartitionSpec as P

HEAD = 64


NEGATIVE = -1e30
EPSILON = 1e-12


def layer_norm(values, gain, shift):
    mean = jnp.mean(values, axis=-1, keepdims=True)
    centred = values - mean
    spread = jnp.mean(centred * centred, axis=-1, keepdims=True)
    return centred * lax.rsqrt(spread + EPSILON) * gain + shift


def gelu_exact(values):
    return jax.nn.gelu(values, approximate=False)


def token_keep(lengths, live, length):
    slots = lengths.shape[0]
    alive = jnp.arange(slots, dtype=jnp.int32) < live
    position = jnp.arange(length, dtype=jnp.int32)
    keep = (position[None, :] < lengths[:, None]) & alive[:, None]
    return keep.astype(jnp.float32)


def masked_scores(query, keyed, keep):
    raw = jnp.einsum("sqhd,skhd->shqk", query, keyed, preferred_element_type=jnp.float32)
    raw = raw * query.shape[-1] ** (-0.5)
    return jnp.where(keep[:, None, None, :] > 0, raw, NEGATIVE)


def attend(query, keyed, valued, keep):
    scores = masked_scores(query, keyed, keep)
    highest = jnp.max(scores, axis=-1, keepdims=True)
    expo = jnp.exp(scores - highest)
    total = jnp.sum(expo, axis=-1, keepdims=True)
    probs = (expo / total).astype(jnp.bfloat16)
    context = jnp.einsum("shqk,skhd->sqhd", probs, valued, preferred_element_type=jnp.float32)
    return (context.astype(jnp.bfloat16), highest + jnp.log(total))


def attend_back(query, keyed, valued, keep, logsum, dcontext):
    scale = query.shape[-1] ** (-0.5)
    scores = masked_scores(query, keyed, keep)
    probs = jnp.exp(scores - logsum)
    dprobs = jnp.einsum("sqhd,skhd->shqk", dcontext, valued, preferred_element_type=jnp.float32)
    inner = jnp.sum(dprobs * probs, axis=-1, keepdims=True)
    dscores = (probs * (dprobs - inner)).astype(jnp.bfloat16)
    query_back = (
        jnp.einsum("shqk,skhd->sqhd", dscores, keyed, preferred_element_type=jnp.float32) * scale
    )
    key_back = (
        jnp.einsum("shqk,sqhd->skhd", dscores, query, preferred_element_type=jnp.float32) * scale
    )
    value_back = jnp.einsum(
        "shqk,sqhd->skhd", probs.astype(jnp.bfloat16), dcontext, preferred_element_type=jnp.float32
    )
    return (
        query_back.astype(jnp.bfloat16),
        key_back.astype(jnp.bfloat16),
        value_back.astype(jnp.bfloat16),
    )


def shards(
    short_input,
    long_input,
    query_weight,
    query_bias,
    key_weight,
    value_weight,
    value_bias,
    output_weight,
    output_bias,
    gain_one,
    shift_one,
    upward_weight,
    upward_bias,
    downward_weight,
    downward_bias,
    gain_two,
    shift_two,
    short_upstream,
    long_upstream,
    short_lengths,
    long_lengths,
    live_counts,
):
    short_slots, short_length, width = short_input.shape
    long_slots, long_length = (long_input.shape[0], long_input.shape[1])
    local = query_weight.shape[1]
    heads = local // HEAD
    short_rows = short_slots * short_length
    keep_short = token_keep(short_lengths, live_counts[0, 0], short_length)
    keep_long = token_keep(long_lengths, live_counts[0, 1], long_length)
    keep_rows = jnp.concatenate([keep_short.reshape(-1), keep_long.reshape(-1)])
    tokens = jnp.concatenate([short_input.reshape(-1, width), long_input.reshape(-1, width)])
    upstream = jnp.concatenate(
        [short_upstream.reshape(-1, width), long_upstream.reshape(-1, width)]
    )

    def short_heads(matrix):
        return matrix[:short_rows].reshape(short_slots, short_length, heads, HEAD)

    def long_heads(matrix):
        return matrix[short_rows:].reshape(long_slots, long_length, heads, HEAD)

    query = (jnp.dot(tokens, query_weight, preferred_element_type=jnp.float32) + query_bias).astype(
        jnp.bfloat16
    )
    keyed = jnp.dot(tokens, key_weight, preferred_element_type=jnp.float32).astype(jnp.bfloat16)
    valued = (
        jnp.dot(tokens, value_weight, preferred_element_type=jnp.float32) + value_bias
    ).astype(jnp.bfloat16)
    short_context, short_logsum = attend(
        short_heads(query), short_heads(keyed), short_heads(valued), keep_short
    )
    long_context, long_logsum = attend(
        long_heads(query), long_heads(keyed), long_heads(valued), keep_long
    )
    context = jnp.concatenate([short_context.reshape(-1, local), long_context.reshape(-1, local)])
    attn_part = jnp.dot(context, output_weight, preferred_element_type=jnp.float32)
    attn_share = lax.psum(attn_part.astype(jnp.bfloat16), "mp").astype(jnp.float32) + output_bias
    first_sum = tokens.astype(jnp.float32) + attn_share
    hidden_share, norm_one_back = jax.vjp(
        layer_norm, first_sum, gain_one.astype(jnp.float32), shift_one.astype(jnp.float32)
    )
    hidden_share_low = hidden_share.astype(jnp.bfloat16)
    pre = jnp.dot(hidden_share_low, upward_weight, preferred_element_type=jnp.float32) + upward_bias
    active, gelu_back = jax.vjp(gelu_exact, pre)
    active_low = active.astype(jnp.bfloat16)
    ffn_part = jnp.dot(active_low, downward_weight, preferred_element_type=jnp.float32)
    ffn_share = lax.psum(ffn_part.astype(jnp.bfloat16), "mp").astype(jnp.float32) + downward_bias
    second_sum = hidden_share + ffn_share

    def final_norm(values, gain, shift):
        return layer_norm(values, gain, shift) * keep_rows[:, None]

    output_share, norm_two_back = jax.vjp(
        final_norm, second_sum, gain_two.astype(jnp.float32), shift_two.astype(jnp.float32)
    )
    output_low = output_share.astype(jnp.bfloat16)
    dsecond, gaintwo_part, shifttwo_part = norm_two_back(upstream.astype(jnp.float32))
    dfed_share = dsecond.astype(jnp.bfloat16)
    downbias_part = jnp.sum(dfed_share, axis=0, dtype=jnp.float32)
    downward_part = jnp.einsum(
        "rf,rd->fd", active_low, dfed_share, preferred_element_type=jnp.float32
    )
    dactive = jnp.einsum(
        "rd,fd->rf", dfed_share, downward_weight, preferred_element_type=jnp.float32
    )
    (dpre,) = gelu_back(dactive)
    dpre_low = dpre.astype(jnp.bfloat16)
    upbias_part = jnp.sum(dpre_low, axis=0, dtype=jnp.float32)
    upward_part = jnp.einsum(
        "rd,rf->df", hidden_share_low, dpre_low, preferred_element_type=jnp.float32
    )
    hidden_part = jnp.einsum(
        "rf,df->rd", dpre_low, upward_weight, preferred_element_type=jnp.float32
    )
    dhidden = dsecond + lax.psum(hidden_part.astype(jnp.bfloat16), "mp").astype(jnp.float32)
    dfirst, gainone_part, shiftone_part = norm_one_back(dhidden)
    dattn_share = dfirst.astype(jnp.bfloat16)
    outbias_part = jnp.sum(dattn_share, axis=0, dtype=jnp.float32)
    output_part = jnp.einsum("rc,rd->cd", context, dattn_share, preferred_element_type=jnp.float32)
    dcontext = jnp.einsum(
        "rd,cd->rc", dattn_share, output_weight, preferred_element_type=jnp.float32
    ).astype(jnp.bfloat16)
    short_back = attend_back(
        short_heads(query),
        short_heads(keyed),
        short_heads(valued),
        keep_short,
        short_logsum,
        short_heads(dcontext),
    )
    long_back = attend_back(
        long_heads(query),
        long_heads(keyed),
        long_heads(valued),
        keep_long,
        long_logsum,
        long_heads(dcontext),
    )
    query_back = jnp.concatenate(
        [short_back[0].reshape(-1, local), long_back[0].reshape(-1, local)]
    )
    key_back = jnp.concatenate([short_back[1].reshape(-1, local), long_back[1].reshape(-1, local)])
    value_back = jnp.concatenate(
        [short_back[2].reshape(-1, local), long_back[2].reshape(-1, local)]
    )
    querybias_part = jnp.sum(query_back, axis=0, dtype=jnp.float32)
    valuebias_part = jnp.sum(value_back, axis=0, dtype=jnp.float32)
    query_part = jnp.einsum("rd,rc->dc", tokens, query_back, preferred_element_type=jnp.float32)
    key_part = jnp.einsum("rd,rc->dc", tokens, key_back, preferred_element_type=jnp.float32)
    value_part = jnp.einsum("rd,rc->dc", tokens, value_back, preferred_element_type=jnp.float32)
    input_part = jnp.einsum(
        "rc,dc->rd", query_back, query_weight, preferred_element_type=jnp.float32
    )
    input_part = input_part + jnp.einsum(
        "rc,dc->rd", key_back, key_weight, preferred_element_type=jnp.float32
    )
    input_part = input_part + jnp.einsum(
        "rc,dc->rd", value_back, value_weight, preferred_element_type=jnp.float32
    )
    input_total = dfirst + lax.psum(input_part.astype(jnp.bfloat16), "mp").astype(jnp.float32)
    norm_grads = (gainone_part, shiftone_part, gaintwo_part, shifttwo_part)
    input_low = input_total.astype(jnp.bfloat16)
    reduced = (
        lax.psum_scatter(query_part, "dp", scatter_dimension=0, tiled=True),
        lax.psum_scatter(key_part, "dp", scatter_dimension=0, tiled=True),
        lax.psum_scatter(value_part, "dp", scatter_dimension=0, tiled=True),
        lax.psum_scatter(output_part, "dp", scatter_dimension=1, tiled=True),
        lax.psum_scatter(upward_part, "dp", scatter_dimension=0, tiled=True),
        lax.psum_scatter(downward_part, "dp", scatter_dimension=1, tiled=True),
        lax.psum_scatter(querybias_part, "dp", scatter_dimension=0, tiled=True),
        lax.psum_scatter(valuebias_part, "dp", scatter_dimension=0, tiled=True),
        lax.psum_scatter(outbias_part, "dp", scatter_dimension=0, tiled=True),
        lax.psum_scatter(upbias_part, "dp", scatter_dimension=0, tiled=True),
        lax.psum_scatter(downbias_part, "dp", scatter_dimension=0, tiled=True),
        lax.psum_scatter(norm_grads[0], "dp", scatter_dimension=0, tiled=True),
        lax.psum_scatter(norm_grads[1], "dp", scatter_dimension=0, tiled=True),
        lax.psum_scatter(norm_grads[2], "dp", scatter_dimension=0, tiled=True),
        lax.psum_scatter(norm_grads[3], "dp", scatter_dimension=0, tiled=True),
    )
    short_output = output_low[:short_rows].reshape(short_input.shape)
    long_output = output_low[short_rows:].reshape(long_input.shape)
    short_inputgrad = input_low[:short_rows].reshape(short_input.shape)
    long_inputgrad = input_low[short_rows:].reshape(long_input.shape)
    return (
        short_output,
        long_output,
        short_inputgrad,
        long_inputgrad,
        reduced[0],
        reduced[6],
        reduced[1],
        reduced[2],
        reduced[7],
        reduced[3],
        reduced[8],
        reduced[11],
        reduced[12],
        reduced[4],
        reduced[9],
        reduced[5],
        reduced[10],
        reduced[13],
        reduced[14],
    )


def solution(mesh):
    in_specs = (
        P("dp", None, None),
        P("dp", None, None),
        P(None, "mp"),
        P("mp"),
        P(None, "mp"),
        P(None, "mp"),
        P("mp"),
        P("mp", None),
        P(),
        P(),
        P(),
        P(None, "mp"),
        P("mp"),
        P("mp", None),
        P(),
        P(),
        P(),
        P("dp", None, None),
        P("dp", None, None),
        P("dp"),
        P("dp"),
        P("dp", None),
    )
    out_specs = (
        P("dp", None, None),
        P("dp", None, None),
        P("dp", None, None),
        P("dp", None, None),
        P("dp", "mp"),
        P(("mp", "dp")),
        P("dp", "mp"),
        P("dp", "mp"),
        P(("mp", "dp")),
        P("mp", "dp"),
        P("dp"),
        P("dp"),
        P("dp"),
        P("dp", "mp"),
        P(("mp", "dp")),
        P("mp", "dp"),
        P("dp"),
        P("dp"),
        P("dp"),
    )
    return jax.shard_map(shards, mesh=mesh, in_specs=in_specs, out_specs=out_specs, check_vma=False)
```

profile of v0, /device:TPU:0, one launch (start us, length us, event | category | flops | bytes accessed | tf_op | source)
XLA Modules:
  0.0 1020.5 jit_solution(16553638569556597942)
XLA Ops:
  11.4 2.4 add_convert_fusion.6
  15.5 2.1 add_convert_fusion.5
  18.4 2.0 reshape.351
  20.4 2.1 convolution_convert_fusion.4
  23.5 1.8 reshape.352
  25.4 1.7 fusion.78
  29.3 1.5 fusion.77
  31.8 1.7 copy-done.1
  35.5 2.1 convolution_convert_fusion
  38.3 22.6 %all-reduce.15.cloned.1.call-done = bf16[1024,768]{1,0:T(8,128)(2,1)} async-done(((bf16[1024,768]{1,0:T(8,128)(2,1)}), bf16[1024,768]{1,0:T(8,128)(2,1)}) %all-reduce.15.cloned.1.call-update) | async-done | bytes 1572880 | tf_op jit(solution)/shard_map/psum | solution.py:129
  60.9 2.3 fusion.15
  64.2 18.5 %multiply_convert_fusion.1 = (bf16[1024,1536]{1,0:T(8,128)(2,1)S(1)}, f32[1024,1536]{1,0:T(8,128)}, f32[1024,1536]{1,0:T(8,128)}) fusion(f32[1536]{0:T(1024)S(1)} %convert_element_type.231, bf16[768,1536]{1,0:T(8,128)(2,1)S(1)} %copy-done, f32[768]{0:T(1024)S(1)} %convert_element_type.229, f32[768]{0:T(1024)S(1)} %convert_element_type.228, ...), kind=kOutput, calls=%fused_computation.7 | convolution fusion | flops 2529165312 | bytes 21257216 | tf_op jit(solution)/shard_map/dot_general | solution.py:135
  82.7 1.7 copy-done.76
  84.4 3.8 convolution_convert_fusion.2
  88.4 21.6 %all-reduce.17.cloned.1.call-done = bf16[1024,768]{1,0:T(8,128)(2,1)} async-done(((bf16[1024,768]{1,0:T(8,128)(2,1)}), bf16[1024,768]{1,0:T(8,128)(2,1)}) %all-reduce.17.cloned.1.call-update) | async-done | bytes 1572880 | tf_op jit(solution)/shard_map/psum | solution.py:139
  110.0 4.0 fusion.70
  115.4 2.9 multiply_reduce_fusion.1
  118.3 3.4 fusion.69
  121.7 1.7 copy-done.2
  124.5 5.1 convert_reduce_fusion
  129.6 1.7 copy-done.75
  131.3 3.8 convolution_convert_fusion.1
  135.8 21.0 %all-reduce.19.cloned.1.call-done = bf16[1024,768]{1,0:T(8,128)(2,1)} async-done(((bf16[1024,768]{1,0:T(8,128)(2,1)}), bf16[1024,768]{1,0:T(8,128)(2,1)}) %all-reduce.19.cloned.1.call-update) | async-done | bytes 1572880 | tf_op jit(solution)/shard_map/psum | solution.py:167
  156.8 5.6 multiply_reduce_fusion.2
  162.5 3.2 fusion.68
  170.1 2.9 fusion.29
  173.1 1.6 multiply_reduce_fusion.7
  175.1 1.4 fusion.26
  177.6 3.9 fusion.22
  181.6 1.3 multiply_reduce_fusion
  182.9 1.9 multiply_convert_fusion
  184.8 2.1 fusion.21
  191.0 2.3 add_convert_fusion.2
  193.6 3.7 fusion.35
  197.4 3.3 fusion.45
  200.8 3.4 fusion.33
  204.3 3.4 fusion.46
  207.8 7.8 fusion.61
  215.7 7.2 fusion.79
  226.2 2.7 slice_bitcast_fusion.1
  229.9 77.7 %all-reduce.9 = (f32[384]{0:T(512)S(1)}, f32[384]{0:T(512)S(1)}, f32[768]{0:T(1024)S(1)}, f32[768]{0:T(1024)S(1)}, f32[768]{0:T(1024)S(1)}, /*index=5*/f32[1536]...) all-reduce(f32[384]{0:T(512)S(1)} %convert_reduce_fusion.4, ...), channel_id=3, replica_groups=mesh['dp'=16,'mp'=2] {'dp'}, use_global_device_ids=true, to_apply=%region_20.21.clone | all-reduce | flops 6912 | bytes 55296
  312.8 2.9 add_convert_fusion.1
  317.0 28.1 %reduce-scatter.13.cloned.1.call-done = f32[384,48]{0,1:T(8,128)} async-done(((f32[384,768]{0,1:T(8,128)}), f32[384,48]{0,1:T(8,128)}) %reduce-scatter.13.cloned.1.call-update) | async-done | bytes 73744 | tf_op jit(solution)/shard_map/reduce_scatter | solution.py:219
  345.1 127.9 %reduce-scatter.11.cloned.1.call-done = f32[48,384]{1,0:T(8,128)} async-done(((f32[768,384]{1,0:T(8,128)}), f32[48,384]{1,0:T(8,128)}) %reduce-scatter.11.cloned.1.call-update) | async-done | bytes 73744 | tf_op jit(solution)/shard_map/reduce_scatter | solution.py:218
  473.0 127.9 %reduce-scatter.9.cloned.1.call-done = f32[48,384]{1,0:T(8,128)} async-done(((f32[768,384]{1,0:T(8,128)}), f32[48,384]{1,0:T(8,128)}) %reduce-scatter.9.cloned.1.call-update) | async-done | bytes 73744 | tf_op jit(solution)/shard_map/reduce_scatter | solution.py:217
  600.9 128.0 %reduce-scatter.7.cloned.1.call-done = f32[48,384]{1,0:T(8,128)} async-done(((f32[768,384]{1,0:T(8,128)}), f32[48,384]{1,0:T(8,128)}) %reduce-scatter.7.cloned.1.call-update) | async-done | bytes 73744 | tf_op jit(solution)/shard_map/reduce_scatter | solution.py:216
  728.9 142.2 %reduce-scatter.15.cloned.1.call-done = f32[48,1536]{1,0:T(8,128)} async-done(((f32[768,1536]{1,0:T(8,128)}), f32[48,1536]{1,0:T(8,128)}) %reduce-scatter.15.cloned.1.call-update) | async-done | bytes 294928 | tf_op jit(solution)/shard_map/reduce_scatter | solution.py:220
  871.1 142.3 %reduce-scatter.17.cloned.1.call-done = f32[1536,48]{0,1:T(8,128)} async-done(((f32[1536,768]{0,1:T(8,128)}), f32[1536,48]{0,1:T(8,128)}) %reduce-scatter.17.cloned.1.call-update) | async-done | bytes 294928 | tf_op jit(solution)/shard_map/reduce_scatter | solution.py:221
  (252 shorter events, 35.0 us)
Async XLA Ops:
  7.2 57.0 %copy-start = (bf16[768,1536]{1,0:T(8,128)(2,1)S(1)}, bf16[768,1536]{1,0:T(8,128)(2,1)}, u32[]{:S(2)}) copy-start(bf16[768,1536]{1,0:T(8,128)(2,1)} %param.33) | copy-start | bytes 7077892
  7.2 53.7 %all-reduce.15.cloned.1.call-start = ((), (), s32[]{:S(2)}) async-start(), calls=%async_computation.6 | async-start | bytes 3145728 | tf_op jit(solution)/shard_map/psum | solution.py:129
  11.4 4.1 copy-start.9
  18.4 10.9 %copy-start.16 = (bf16[512,384]{0,1:T(8,128)(2,1)}, bf16[512,384]{0,1:T(8,128)(2,1)S(1)}, u32[]{:S(2)}) copy-start(bf16[512,384]{0,1:T(8,128)(2,1)S(1)} %get-tuple-element.58) | copy-start | bytes 1179652
  20.4 4.9 copy-start.69
  28.6 6.1 copy-start.40
  37.7 72.3 %all-reduce.17.cloned.1.call-start = ((), (), s32[]{:S(2)}) async-start(), calls=%async_computation.7 | async-start | bytes 3145728 | tf_op jit(solution)/shard_map/psum | solution.py:139
  38.2 124.3 %copy-start.42 = (f32[768]{0:T(1024)}, f32[768]{0:T(1024)S(1)}, u32[]{:S(2)}) copy-start(f32[768]{0:T(1024)S(1)} %convert_element_type.227) | copy-start | bytes 9220
  38.2 124.2 %copy-start.48 = (f32[768]{0:T(1024)}, f32[768]{0:T(1024)S(1)}, u32[]{:S(2)}) copy-start(f32[768]{0:T(1024)S(1)} %convert_element_type.228) | copy-start | bytes 9220
  38.3 71.7 %copy-start.61 = (f32[768]{0:T(1024)}, f32[768]{0:T(1024)S(1)}, u32[]{:S(2)}) copy-start(f32[768]{0:T(1024)S(1)} %convert_element_type.229) | copy-start | bytes 9220
  63.3 99.2 %copy-start.46 = (f32[1024]{0:T(1024)}, f32[1024]{0:T(1024)S(1)}, u32[]{:S(2)}) copy-start(f32[1024]{0:T(1024)S(1)} %broadcast_multiply_fusion.1) | copy-start | bytes 12292
  64.2 98.3 %copy-start.50 = (f32[1024]{0:T(1024)}, f32[1024]{0:T(1024)S(1)}, u32[]{:S(2)}) copy-start(f32[1024]{0:T(1024)S(1)} %fusion.48) | copy-start | bytes 12292
  64.2 20.2 %copy-start.70 = (bf16[1536,768]{1,0:T(8,128)(2,1)S(1)}, bf16[1536,768]{1,0:T(8,128)(2,1)}, u32[]{:S(2)}) copy-start(bf16[1536,768]{1,0:T(8,128)(2,1)} %param.35) | copy-start | bytes 7077892
  84.4 3.8 copy-start.66
  84.4 3.9 copy-start.67
  84.4 3.9 copy-start.68
  88.2 68.6 %all-reduce.19.cloned.1.call-start = ((), (), s32[]{:S(2)}) async-start(), calls=%async_computation.8 | async-start | bytes 3145728 | tf_op jit(solution)/shard_map/psum | solution.py:167
  110.0 14.4 %slice-start.4 = ((s8[6291456]{0:T(1024)(128)(4,1)}), s8[4194304]{0:T(1024)(128)(4,1)S(1)}, s32[]{:S(2)}) async-start(s8[6291456]{0:T(1024)(128)(4,1)} %bitcast.186), calls=%async_computation.20 | async-start | bytes 8388608
  115.4 9.0 slice-start.5
  118.3 6.0 slice-start.2
  118.3 6.0 slice-start.3
  124.3 5.2 copy-start.33
  131.3 3.9 copy-start.53
  131.3 3.9 copy-start.55
  131.3 3.9 copy-start.45
  135.1 177.7 %all-reduce.21.cloned.1.call-start = ((), (), s32[]{:S(2)}) async-start(), calls=%async_computation.9 | async-start | bytes 3145728 | tf_op jit(solution)/shard_map/psum | solution.py:212
  156.8 5.7 copy-start.3
  156.8 5.7 copy-start.5
  156.8 5.7 copy-start.11
  156.8 5.7 copy-start.12
  174.7 6.8 slice-start
  176.5 5.0 slice-start.1
  177.6 3.9 copy-start.26
  193.4 151.7 %reduce-scatter.13.cloned.1.call-start = ((), (), s32[]{:S(2)}) async-start(), calls=%async_computation.13 | async-start | bytes 1253376 | tf_op jit(solution)/shard_map/reduce_scatter | solution.py:219
  197.4 275.7 %reduce-scatter.11.cloned.1.call-start = ((), (), s32[]{:S(2)}) async-start(), calls=%async_computation.12 | async-start | bytes 1253376 | tf_op jit(solution)/shard_map/reduce_scatter | solution.py:218
  200.7 400.2 %reduce-scatter.9.cloned.1.call-start = ((), (), s32[]{:S(2)}) async-start(), calls=%async_computation.11 | async-start | bytes 1253376 | tf_op jit(solution)/shard_map/reduce_scatter | solution.py:217
  204.2 3.6 copy-start.43
  204.2 3.6 copy-start.47
  204.2 3.6 copy-start.49
  204.3 524.7 %reduce-scatter.7.cloned.1.call-start = ((), (), s32[]{:S(2)}) async-start(), calls=%async_computation.10 | async-start | bytes 1253376 | tf_op jit(solution)/shard_map/reduce_scatter | solution.py:216
  207.7 663.4 %reduce-scatter.15.cloned.1.call-start = ((), (), s32[]{:S(2)}) async-start(), calls=%async_computation.14 | async-start | bytes 5013504 | tf_op jit(solution)/shard_map/reduce_scatter | solution.py:220
  215.6 797.8 %reduce-scatter.17.cloned.1.call-start = ((), (), s32[]{:S(2)}) async-start(), calls=%async_computation.15 | async-start | bytes 5013504 | tf_op jit(solution)/shard_map/reduce_scatter | solution.py:221
  222.9 6.0 copy-start.14
  222.9 6.8 copy-start.20
  222.9 6.9 copy-start.58
  222.9 6.9 copy-start.59
  222.9 6.9 copy-start.60
  222.9 89.9 %copy-start.57 = (f32[1024]{0:T(1024)S(1)}, f32[1024]{0:T(1024)}, u32[]{:S(2)}) copy-start(f32[1024]{0:T(1024)} %copy-done.56) | copy-start | bytes 12292
  (45 other events, 98.3 us)
Sparse Core Ops, SparseCore 0:
  37.8 23.1 all-reduce.14
  88.3 21.5 all-reduce.16
  135.2 21.5 all-reduce.18
  193.5 21.5 all-reduce.20
  220.3 124.7 reduce-scatter.12
  350.3 122.7 reduce-scatter.10
  478.4 122.5 reduce-scatter.8
  606.3 122.6 reduce-scatter.6
  734.7 136.4 reduce-scatter.14
  877.5 135.8 reduce-scatter.16
where the time goes:
time: 1030 us; the launch traced here: 1020 us
  waiting for transfers between devices  762 us (74%)
  matrix products  93.7 us (9%)
  blocking collectives  77.7 us (8%)
  other arithmetic  34.8 us (3%)
  local copies, waits for them, and re-layouts  32.3 us (3%)
  between operations  19 us (2%)
    reduce_scatter x1, waiting for transfers between devices, shards(): lax.psum_scatter(downward_part, 'dp', scatter_dimension=1, tiled=True)  142 us
    reduce_scatter x1, waiting for transfers between devices, shards(): lax.psum_scatter(upward_part, 'dp', scatter_dimension=0, tiled=True)  142 us
    reduce_scatter x1, waiting for transfers between devices, shards(): lax.psum_scatter(query_part, 'dp', scatter_dimension=0, tiled=True)  128 us
    reduce_scatter x1, waiting for transfers between devices, shards(): lax.psum_scatter(value_part, 'dp', scatter_dimension=0, tiled=True)  128 us
    reduce_scatter x1, waiting for transfers between devices, shards(): lax.psum_scatter(key_part, 'dp', scatter_dimension=0, tiled=True)  128 us
    unnamed x1, blocking collectives  77.7 us
    reduce_scatter x1, waiting for transfers between devices, shards(): lax.psum_scatter(output_part, 'dp', scatter_dimension=1, tiled=True)  28.1 us
    psum x1, waiting for transfers between devices, shards(): lax.psum(attn_part.astype(jnp.bfloat16), 'mp').astype(jnp.float32)  22.6 us
  transfers between devices with their start and end apart: 10, of which 9 were waited for; matrix products, arithmetic and copies ran while one was open for 4% of the time, Pallas kernels for 0%

commit v1 on v0

v1 whole, which is shorter than its diff:
```python
import functools

import jax
import jax.numpy as jnp
from jax import lax
from jax.experimental import pallas as pl
from jax.experimental.pallas import tpu as pltpu
from jax.sharding import PartitionSpec as P

HEAD = 64
PAIR = 2 * HEAD
NEGATIVE = -1e30
EPSILON = 1e-12
BF = jnp.bfloat16
F32 = jnp.float32
MESH = pl.DeviceIdType.MESH

BITS = 4
X, Y, NEAR, FAR = 0, 1, 2, 3
ORDERS = ((X, Y, NEAR, FAR), (Y, NEAR, X, FAR), (NEAR, X, Y, FAR))
KINDS = (0, 1, 2, 0, 1, 2, 0, 1, 2, 0, 1, 0)
PARTS_AT = (0, 8, 12, 14)


def mm(left, right):
    return jnp.dot(left, right, preferred_element_type=F32)


def mm_nt(left, right):
    return lax.dot_general(left, right, (((1,), (1,)), ((), ())), preferred_element_type=F32)


def mm_tn(left, right):
    return lax.dot_general(left, right, (((0,), (0,)), ((), ())), preferred_element_type=F32)


def rows_of(start, size):
    return pl.ds(pl.multiple_of(start, size), size)


def fold(values):
    rows, width = values.shape
    return jnp.sum(values.reshape(rows // 8, 8, width), axis=0)


def place(order, block):
    spot = 0
    for bit in order:
        spot = spot * 2 + ((block >> bit) & 1)
    return spot


class Refs:
    pass


def layer(reduce_here, names, *refs):
    r = Refs()
    for name, ref in zip(names, refs, strict=True):
        setattr(r, name, ref)
    dp, mp = lax.axis_index("dp"), lax.axis_index("mp")
    peer = (dp, 1 - mp)
    half = r.own.shape[1]
    seg_rows = 2 * half
    width = r.x.shape[1]
    local = r.q.shape[1]
    pairs = local // PAIR
    hidden = r.f.shape[1]
    short_slots, short_length = r.xs.shape[0], r.xs.shape[1]
    long_length = r.xl.shape[1]
    chunk = r.G.shape[3]
    block = r.G.shape[2]
    tile = 64

    my_bit = [lax.rem(lax.div(dp, 1 << k), 2) for k in range(BITS)]
    across = [(dp + (1 - 2 * my_bit[k]) * (1 << k), mp) for k in range(BITS)]

    loads = {}

    def load(name, src, dst):
        cp = pltpu.make_async_copy(src, dst, r.load_sem.at[len(loads)])
        cp.start()
        loads[name] = cp

    load("xl", r.xl.at[0], r.x.at[pl.ds(seg_rows, seg_rows)])
    load("wq", r.wq_h, r.wq)
    load("wk", r.wk_h, r.wk)
    load("wv", r.wv_h, r.wv)
    for s in range(short_slots):
        load(f"xs{s}", r.xs.at[s], r.x.at[pl.ds(s * short_length, short_length)])
    load("wo", r.wo_h, r.wo)
    load("wu", r.wu_h, r.wu)
    load("wd", r.wd_h, r.wd)
    load("us", r.us.at[pl.ds(mp * (short_slots // 2), short_slots // 2)], r.ups)
    load("ul", r.ul.at[0, rows_of(mp * half, half)], r.upl)

    barrier = pltpu.get_barrier_semaphore()
    partners = [peer] + (across if reduce_here else [])
    for other in partners:
        pl.semaphore_signal(barrier, inc=1, device_id=other, device_id_type=MESH)

    sends = []

    def remote(src, dst, index, device):
        cp = pltpu.make_async_remote_copy(
            src_ref=src,
            dst_ref=dst,
            send_sem=r.ex_send.at[index],
            recv_sem=r.ex_recv.at[index],
            device_id=device,
            device_id_type=MESH,
        )
        cp.start()
        sends.append(cp)
        return cp

    live_short, live_long = r.live[0, 0], r.live[0, 1]
    long_len = jnp.where(live_long > 0, r.ll[0], 0)

    def short_len(slot):
        return jnp.where(slot < live_short, r.sl[slot], 0)

    def param(ref):
        return ref[...].astype(F32).reshape(1, -1)

    qb, vb, ob, g1, b1 = (param(n) for n in (r.qb, r.vb, r.ob, r.g1, r.b1))
    ub, db, g2, b2 = (param(n) for n in (r.ub, r.db, r.g2, r.b2))

    low_lane = lax.broadcasted_iota(jnp.int32, (1, PAIR), 1) < HEAD

    def first(values):
        return jnp.where(low_lane, values, jnp.zeros_like(values))

    def second(values):
        return jnp.where(low_lane, jnp.zeros_like(values), values)

    def own_start(seg):
        return seg * seg_rows + mp * half

    def peer_start(seg):
        return seg * seg_rows + (1 - mp) * half

    r.acc[...] = jnp.zeros_like(r.acc)
    r.acc_up[...] = jnp.zeros_like(r.acc_up)
    r.acc_qv[...] = jnp.zeros_like(r.acc_qv)

    def project(seg):
        rows = slice(seg * seg_rows, (seg + 1) * seg_rows)
        tokens = r.x[rows, :]
        r.q[rows, :] = (mm(tokens, r.wq[...]) + qb).astype(BF) * BF(HEAD**-0.5)
        r.k[rows, :] = mm(tokens, r.wk[...]).astype(BF)
        r.v[rows, :] = (mm(tokens, r.wv[...]) + vb).astype(BF)

    def softmax(scores):
        highest = jnp.max(scores, axis=-1, keepdims=True)
        expo = jnp.exp(scores - highest)
        total = jnp.sum(expo, axis=-1, keepdims=True)
        return (expo * (1.0 / total)).astype(BF)

    def attend(rows, keys, bias, pair, store):
        lanes = slice(pair * PAIR, (pair + 1) * PAIR)
        qp, kp, vp = r.q[rows, lanes], r.k[keys, lanes], r.v[keys, lanes]
        p0 = softmax(mm_nt(first(qp), kp) + bias)
        p1 = softmax(mm_nt(second(qp), kp) + bias)
        store(2 * pair, p0)
        store(2 * pair + 1, p1)
        r.ctx[rows, lanes] = jnp.where(low_lane, mm(p0, vp), mm(p1, vp)).astype(BF)

    def attend_long():
        tq = 128
        position = lax.broadcasted_iota(jnp.int32, (1, long_length), 1)
        bias = jnp.where(position < long_len, 0.0, NEGATIVE)
        keys = slice(seg_rows, 2 * seg_rows)

        @pl.loop(0, long_length // tq)
        def _(t):
            def store(head, probs):
                r.pl[head, rows_of(t * tq, tq), :] = probs

            for pair in range(pairs):
                attend(rows_of(seg_rows + t * tq, tq), keys, bias, pair, store)

    def attend_short():
        position = lax.broadcasted_iota(jnp.int32, (1, short_length), 1)

        @pl.loop(0, short_slots)
        def _(s):
            bias = jnp.where(position < short_len(s), 0.0, NEGATIVE)
            rows = rows_of(s * short_length, short_length)

            def store(head, probs):
                r.ps[s, head] = probs

            for pair in range(pairs):
                attend(rows, rows, bias, pair, store)

    def exchange(stage, seg, left, right, product):
        index = 2 * stage + seg
        r.out_buf[index] = product(left[rows_of(peer_start(seg), half), :], right[...]).astype(BF)
        cp = remote(r.out_buf.at[index], r.in_buf.at[index], index, peer)
        r.own[seg] = product(left[rows_of(own_start(seg), half), :], right[...])
        return cp

    def share(index, seg, ref):
        rows = rows_of(own_start(seg), half)
        return remote(ref.at[rows], ref.at[rows], index, peer)

    def norm(values):
        mean = jnp.mean(values, axis=-1, keepdims=True)
        centred = values - mean
        scale = lax.rsqrt(jnp.mean(centred * centred, axis=-1, keepdims=True) + EPSILON)
        return centred * scale, scale

    def norm_back(normed, scale, grad):
        return scale * (
            grad
            - jnp.mean(grad, axis=-1, keepdims=True)
            - normed * jnp.mean(grad * normed, axis=-1, keepdims=True)
        )

    def norm_one(seg):
        @pl.loop(0, half // tile)
        def _(t):
            mine = rows_of(seg * half + t * tile, tile)
            here = rows_of(t * tile, tile)
            rows = rows_of(own_start(seg) + t * tile, tile)
            total = r.own[seg, here, :] + r.in_buf[seg, here, :].astype(F32) + ob
            normed, scale = norm(r.x[rows, :].astype(F32) + total)
            r.n1[mine, :] = normed
            r.r1[mine, :] = scale
            r.h[rows, :] = (normed * g1 + b1).astype(BF)

    def up(start):
        rows = rows_of(start, half)
        step = 512
        for j in range(hidden // step):
            cols = slice(j * step, (j + 1) * step)
            pre = mm(r.h[rows, :], r.wu[:, cols]) + ub[:, cols]
            phi = 0.5 + 0.5 * lax.erf(pre * (0.5**0.5))
            r.f[rows, cols] = (pre * phi).astype(BF)
            r.gp[rows, cols] = (phi + pre * (jnp.exp(pre * pre * -0.5) * 0.3989422804014327)).astype(BF)

    def norm_two(seg):
        @pl.loop(0, half // tile)
        def _(t):
            mine = rows_of(seg * half + t * tile, tile)
            here = rows_of(t * tile, tile)
            rows = rows_of(own_start(seg) + t * tile, tile)
            row = lax.broadcasted_iota(jnp.int32, (tile, 1), 0)
            if seg == 0:
                per_slot = short_length // tile
                slot = lax.div(t, per_slot)
                inner = rows_of(lax.rem(t, per_slot) * tile, tile)
                keep = row + lax.rem(t, per_slot) * tile < short_len(mp * (short_slots // 2) + slot)
                upstream = r.ups[slot, inner, :]
            else:
                keep = row + (mp * half + t * tile) < long_len
                upstream = r.upl[here, :]
            keep = keep.astype(F32)
            hidden_state = r.n1[mine, :] * g1 + b1
            total = r.own[seg, here, :] + r.in_buf[2 + seg, here, :].astype(F32) + db
            normed, scale = norm(hidden_state + total)
            r.out[seg, here, :] = (keep * (normed * g2 + b2)).astype(BF)
            grad = keep * upstream.astype(F32)
            r.acc[0] += fold(grad * normed)
            r.acc[1] += fold(grad)
            dsecond = norm_back(normed, scale, grad * g2)
            low = dsecond.astype(BF)
            r.acc[2] += fold(low.astype(F32))
            r.ds[mine, :] = dsecond
            r.do[rows, :] = low

    def norm_one_back(seg):
        @pl.loop(0, half // tile)
        def _(t):
            mine = rows_of(seg * half + t * tile, tile)
            here = rows_of(t * tile, tile)
            rows = rows_of(own_start(seg) + t * tile, tile)
            grad = r.ds[mine, :] + r.own[seg, here, :] + r.in_buf[4 + seg, here, :].astype(F32)
            normed = r.n1[mine, :]
            r.acc[3] += fold(grad * normed)
            r.acc[4] += fold(grad)
            dfirst = norm_back(normed, r.r1[mine, :], grad * g1)
            low = dfirst.astype(BF)
            r.acc[5] += fold(low.astype(F32))
            r.ds[mine, :] = dfirst
            r.da[rows, :] = low

    def active_back(seg):
        for part in range(2):
            rows = slice(seg * seg_rows + part * half, seg * seg_rows + (part + 1) * half)
            step = 512
            for j in range(hidden // step):
                cols = slice(j * step, (j + 1) * step)
                low = (mm_nt(r.do[rows, :], r.wd[cols, :]) * r.gp[rows, cols].astype(F32)).astype(BF)
                r.acc_up[:, cols] += fold(low.astype(F32))
                r.gp[rows, cols] = low

    def attend_back(rows, keys, pair, probs, dscores):
        lanes = slice(pair * PAIR, (pair + 1) * PAIR)
        kp, vp, dc = r.k[keys, lanes], r.v[keys, lanes], r.dctx[rows, lanes]
        product = dc.astype(F32) * r.ctx[rows, lanes].astype(F32)
        parts = []
        for j, pick in enumerate((first, second)):
            inner = jnp.sum(pick(product), axis=-1, keepdims=True)
            low = (probs(2 * pair + j).astype(F32) * (mm_nt(pick(dc), vp) - inner)).astype(BF)
            dscores(j, low)
            parts.append(mm(low, kp))
        dq = (jnp.where(low_lane, parts[0], parts[1]) * HEAD**-0.5).astype(BF)
        r.dq[rows, lanes] = dq

    def keys_back(rows, pair, probs, dscores):
        lanes = slice(pair * PAIR, (pair + 1) * PAIR)
        qp, dc = r.q[rows, lanes], r.dctx[rows, lanes]
        r.dk[rows, lanes] = jnp.where(low_lane, mm_tn(dscores(0), qp), mm_tn(dscores(1), qp)).astype(BF)
        dv = jnp.where(low_lane, mm_tn(probs(2 * pair), dc), mm_tn(probs(2 * pair + 1), dc))
        r.dv[rows, lanes] = dv.astype(BF)

    def attend_long_back():
        tq = 128
        keys = slice(seg_rows, 2 * seg_rows)
        for pair in range(pairs):

            @pl.loop(0, long_length // tq)
            def _(t, pair=pair):
                here = rows_of(t * tq, tq)

                def store(j, low):
                    r.dS[j, here, :] = low

                attend_back(rows_of(seg_rows + t * tq, tq), keys, pair, lambda head: r.pl[head, here, :], store)

            keys_back(keys, pair, lambda head: r.pl[head], lambda j: r.dS[j])

    def attend_short_back():
        @pl.loop(0, short_slots)
        def _(s):
            rows = rows_of(s * short_length, short_length)
            for pair in range(pairs):
                held = [None, None]

                def store(j, low, held=held):
                    held[j] = low

                attend_back(rows, rows, pair, lambda head: r.ps[s, head], store)
                keys_back(rows, pair, lambda head: r.ps[s, head], lambda j, held=held: held[j])

    begin = {}

    def half_copy(c, p):
        order = ORDERS[KINDS[c]]
        if p == 0:
            begin[c] = 0
        n = 8 >> p
        bit = order[p]
        cp = pltpu.make_async_remote_copy(
            src_ref=r.G.at[c, pl.ds(begin[c] + (1 - my_bit[bit]) * n, n)],
            dst_ref=r.R.at[c, pl.ds(PARTS_AT[p], n)],
            send_sem=r.rs_send.at[c, p],
            recv_sem=r.rs_recv.at[c, p],
            device_id=across[bit],
            device_id_type=MESH,
        )
        cp.start()
        sends.append(cp)
        begin[c] = begin[c] + my_bit[bit] * n
        flight[c] = (p, cp)

    flight = {}

    def gradient(c, left, right):
        order = ORDERS[KINDS[c]] if reduce_here else (3, 2, 1, 0)
        blocks = width // block
        for m in range(2):
            part = width // 2
            piece = mm_tn(left[:, m * part : (m + 1) * part], right).astype(BF)
            for b in range(blocks // 2):
                r.G[c, place(order, m * blocks // 2 + b)] = piece[b * block : (b + 1) * block]
        if reduce_here:
            half_copy(c, 0)

    def advance(c):
        p, cp = flight[c]
        n = 8 >> p
        cp.wait_recv()
        if p < BITS - 1:
            mine = pl.ds(begin[c], n)
            r.G[c, mine] = r.G[c, mine] + r.R[c, PARTS_AT[p] : PARTS_AT[p] + n]
            half_copy(c, p + 1)
        else:
            total = r.G[c, begin[c]].astype(F32) + r.R[c, PARTS_AT[p]].astype(F32)
            ref, at, turned = r.targets[c]
            if turned:
                ref[at * chunk : (at + 1) * chunk, :] = total.T
            else:
                ref[:, at * chunk : (at + 1) * chunk] = total

    ups = hidden // chunk
    if reduce_here:
        r.targets = (
            [(r.gdown, j, True) for j in range(ups)]
            + [(r.gup, j, False) for j in range(ups)]
            + [(r.gout, 0, True), (r.gq, 0, False), (r.gk, 0, False), (r.gv, 0, False)]
        )
    todo = list(EVENTS) if reduce_here else []

    def drain(upto):
        while todo and len(EVENTS) - len(todo) < upto:
            advance(todo.pop(0))

    for name in ("xl", "wq", "wk", "wv"):
        loads[name].wait()
    project(1)
    attend_long()
    for s in range(short_slots):
        loads[f"xs{s}"].wait()
    loads["wo"].wait()
    pl.semaphore_wait(barrier, len(partners))
    ex = {}
    ex["a1"] = exchange(0, 1, r.ctx, r.wo, mm)
    project(0)
    attend_short()
    ex["a0"] = exchange(0, 0, r.ctx, r.wo, mm)
    loads["wu"].wait()
    loads["wd"].wait()
    ex["a1"].wait_recv()
    norm_one(1)
    ex["h1"] = share(8, 1, r.h)
    ex["a0"].wait_recv()
    norm_one(0)
    ex["h0"] = share(9, 0, r.h)
    for seg in (1, 0):
        up(own_start(seg))
        ex[f"h{seg}"].wait_recv()
        up(peer_start(seg))
        ex[f"o{seg}"] = exchange(1, seg, r.f, r.wd, mm)
    loads["us"].wait()
    loads["ul"].wait()
    outs, arrivals = [], []

    def publish(index, seg, short_ref, long_ref, held):
        if seg == 0:
            for s in range(short_slots // 2):
                piece = held.at[0, pl.ds(s * short_length, short_length)]
                target = short_ref.at[mp * (short_slots // 2) + s]
                cp = pltpu.make_async_copy(piece, target, r.out_sem.at[index + s])
                cp.start()
                outs.append(cp)
                arrivals.append(remote(piece, target, 16 + index + s, peer))
        else:
            target = long_ref.at[0, rows_of(mp * half, half)]
            cp = pltpu.make_async_copy(held.at[1], target, r.out_sem.at[index + 2])
            cp.start()
            outs.append(cp)
            arrivals.append(remote(held.at[1], target, 16 + index + 2, peer))

    for seg in (1, 0):
        ex[f"o{seg}"].wait_recv()
        norm_two(seg)
        ex[f"do{seg}"] = share(10 + seg, seg, r.do)
    ex["do1"].wait_recv()
    ex["do0"].wait_recv()

    for j in range(ups):
        gradient(j, r.do, r.f[:, j * chunk : (j + 1) * chunk])
    publish(0, 1, r.os, r.ol, r.out)
    publish(0, 0, r.os, r.ol, r.out)
    active_back(1)
    drain(MARKS[0])
    active_back(0)
    drain(MARKS[1])
    for j in range(ups):
        gradient(ups + j, r.h, r.gp[:, j * chunk : (j + 1) * chunk])
    drain(MARKS[2])
    for seg in (1, 0):
        ex[f"dh{seg}"] = exchange(2, seg, r.gp, r.wu, mm_nt)
    drain(MARKS[3])
    for seg in (1, 0):
        ex[f"dh{seg}"].wait_recv()
        norm_one_back(seg)
        ex[f"da{seg}"] = share(12 + seg, seg, r.da)
    drain(MARKS[4])
    for seg in (1, 0):
        ex[f"da{seg}"].wait_recv()
        rows = slice(seg * seg_rows, (seg + 1) * seg_rows)
        r.dctx[rows, :] = mm_nt(r.da[rows, :], r.wo[...]).astype(BF)
    gradient(2 * ups, r.da, r.ctx[...])
    drain(MARKS[5])
    attend_long_back()
    drain(MARKS[6])
    attend_short_back()
    drain(MARKS[7])
    for j, ref in enumerate((r.dq, r.dk, r.dv)):
        gradient(2 * ups + 1 + j, r.x, ref[...])
    r.acc_qv[:, :local] = fold(r.dq[...].astype(F32))
    r.acc_qv[:, local:] = fold(r.dv[...].astype(F32))
    drain(MARKS[8])

    def total_of(values):
        return jnp.sum(values, axis=0, keepdims=True)

    r.vec[...] = jnp.zeros_like(r.vec)
    r.vec[0:1, :] = total_of(r.acc_qv[...])
    r.vec[1:2, :] = total_of(r.acc_up[:, :width])
    r.vec[2:3, :] = total_of(r.acc_up[:, width:])
    for j in range(6):
        r.vec[8 + j : 9 + j, :] = total_of(r.acc[j])
    r.vec_out[0] = r.vec[...]
    vec_copy = remote(r.vec_out.at[0, pl.ds(8, 8)], r.vec_in.at[0, pl.ds(8, 8)], 14, peer)

    def input_part(rows):
        return (
            mm_nt(r.dq[rows, :], r.wq[...])
            + mm_nt(r.dk[rows, :], r.wk[...])
            + mm_nt(r.dv[rows, :], r.wv[...])
        )

    for seg in (1, 0):
        index = 6 + seg
        r.out_buf[index] = input_part(rows_of(peer_start(seg), half)).astype(BF)
        ex[f"dx{seg}"] = remote(r.out_buf.at[index], r.in_buf.at[index], index, peer)
        r.own[seg] = input_part(rows_of(own_start(seg), half))
    vec_copy.wait_recv()
    r.vec[8:16, :] = r.vec[8:16, :] + r.vec_in[0, 8:16, :]
    drain(MARKS[9])
    if reduce_here:
        r.vec_out[1] = r.vec[...]
        vec_copy = remote(r.vec_out.at[1], r.vec_in.at[1], 15, across[0])
    for seg in (1, 0):
        ex[f"dx{seg}"].wait_recv()
        dfirst = r.ds[seg * half : (seg + 1) * half, :]
        r.dxo[seg] = (dfirst + r.own[seg] + r.in_buf[6 + seg].astype(F32)).astype(BF)
        publish(3, seg, r.dxs, r.dxl, r.dxo)
    if reduce_here:
        drain(MARKS[10])
        for k in range(1, BITS + 1):
            vec_copy.wait_recv()
            r.vec[...] = r.vec[...] + r.vec_in[k]
            if k < BITS:
                r.vec_out[k + 1] = r.vec[...]
                vec_copy = remote(r.vec_out.at[k + 1], r.vec_in.at[k + 1], 21 + k, across[k])
            drain(MARKS[10 + k])
        high = r.vec[...].astype(BF)
        rest = r.vec[...] - high.astype(F32)
        middle = rest.astype(BF)
        last = (rest - middle.astype(F32)).astype(BF)

        def pick(size, offset):
            source = lax.broadcasted_iota(jnp.int32, (width, PAIR), 0)
            target = lax.broadcasted_iota(jnp.int32, (width, PAIR), 1)
            chosen = (source - target == dp * size + offset) & (target < size)
            chosen = chosen.astype(BF)
            return mm(high, chosen) + mm(middle, chosen) + mm(last, chosen)

        shared = pick(block, 0)
        for j, ref in enumerate((r.g_gain2, r.g_shift2, r.g_db, r.g_gain1, r.g_shift1, r.g_ob)):
            ref[...] = shared[8 + j : 9 + j, :block]
        size = r.g_qb.shape[1]
        r.g_qb[...] = pick(size, 0)[0:1, :size]
        r.g_vb[...] = pick(size, local)[0:1, :size]
        size = r.g_ub.shape[1]
        r.g_ub[...] = (pick(size, 0)[1:2, :] + pick(size, -width)[2:3, :])[:, :size]
        drain(len(EVENTS))
    else:
        r.vec_part[...] = r.vec[...]
        cp = pltpu.make_async_copy(r.G, r.grads, r.out_sem.at[6])
        cp.start()
        cp.wait()

    for cp in outs:
        cp.wait()
    for cp in arrivals:
        cp.wait_recv()
    for cp in sends:
        cp.wait_send()


EVENTS = tuple(c for wave in ((0, 1, 2), (3, 4, 5), (6, 7, 8), (9, 10, 11)) for p in range(BITS) for c in wave)
MARKS = (0, 3, 6, 9, 12, 18, 21, 24, 27, 30, 33, 36, 39, 42, 48)


def shards(n_dp, *args):
    (
        xs, xl, wq, qb, wk, wv, vb, wo, ob, g1, b1, wu, ub, wd, db, g2, b2, us, ul, sl, ll, live,
    ) = args
    short_slots, short_length, width = xs.shape
    long_length = xl.shape[1]
    local, hidden = wq.shape[1], wu.shape[1]
    heads = local // HEAD
    rows = short_slots * short_length + xl.shape[0] * long_length
    half = long_length // 2
    reduce_here = n_dp == 1 << BITS
    blocks = 1 << BITS
    block = width // blocks
    chunk = local
    chunks = (4 * local + 2 * hidden) // chunk
    any_spec = pl.BlockSpec(memory_space=pl.ANY)
    vmem = pl.BlockSpec(memory_space=pltpu.VMEM)
    smem = pl.BlockSpec(memory_space=pltpu.SMEM)
    inputs = [
        ("sl", sl, smem), ("ll", ll, smem), ("live", live, smem),
        ("xs", xs, any_spec), ("xl", xl, any_spec), ("us", us, any_spec), ("ul", ul, any_spec),
        ("wq_h", wq, any_spec), ("wk_h", wk, any_spec), ("wv_h", wv, any_spec), ("wo_h", wo, any_spec),
        ("wu_h", wu, any_spec), ("wd_h", wd, any_spec),
        ("qb", qb, vmem), ("vb", vb, vmem), ("ob", ob, vmem), ("g1", g1, vmem), ("b1", b1, vmem),
        ("ub", ub, vmem), ("db", db, vmem), ("g2", g2, vmem), ("b2", b2, vmem),
    ]
    sds = jax.ShapeDtypeStruct
    outputs = [
        ("os", sds(xs.shape, BF), any_spec), ("ol", sds(xl.shape, BF), any_spec),
        ("dxs", sds(xs.shape, BF), any_spec), ("dxl", sds(xl.shape, BF), any_spec),
    ]
    if reduce_here:
        for name, shape in (
            ("gq", (block, local)), ("gk", (block, local)), ("gv", (block, local)), ("gout", (local, block)),
            ("gup", (block, hidden)), ("gdown", (hidden, block)),
            ("g_qb", (1, local // blocks)), ("g_vb", (1, local // blocks)), ("g_ub", (1, hidden // blocks)),
            ("g_ob", (1, block)), ("g_gain1", (1, block)), ("g_shift1", (1, block)),
            ("g_db", (1, block)), ("g_gain2", (1, block)), ("g_shift2", (1, block)),
        ):
            outputs.append((name, sds(shape, F32), vmem))
    else:
        outputs.append(("grads", sds((chunks, blocks, block, chunk), BF), any_spec))
        outputs.append(("vec_part", sds((16, width), F32), vmem))
    v = pltpu.VMEM
    dma = pltpu.SemaphoreType.DMA
    scratch = [
        ("x", v((rows, width), BF)), ("ups", v((short_slots // 2, short_length, width), BF)), ("upl", v((half, width), BF)),
        ("wq", v(wq.shape, BF)), ("wk", v(wk.shape, BF)), ("wv", v(wv.shape, BF)), ("wo", v(wo.shape, BF)),
        ("wu", v(wu.shape, BF)), ("wd", v(wd.shape, BF)),
        ("q", v((rows, local), BF)), ("k", v((rows, local), BF)), ("v", v((rows, local), BF)),
        ("pl", v((heads, long_length, long_length), BF)), ("ps", v((short_slots, heads, short_length, short_length), BF)),
        ("ctx", v((rows, local), BF)), ("n1", v((2 * half, width), F32)), ("r1", v((2 * half, 1), F32)),
        ("h", v((rows, width), BF)), ("f", v((rows, hidden), BF)), ("gp", v((rows, hidden), BF)),
        ("do", v((rows, width), BF)), ("ds", v((2 * half, width), F32)), ("da", v((rows, width), BF)),
        ("dctx", v((rows, local), BF)), ("dq", v((rows, local), BF)), ("dk", v((rows, local), BF)), ("dv", v((rows, local), BF)),
        ("dS", v((2, long_length, long_length), BF)),
        ("G", v((chunks, blocks, block, chunk), BF)), ("R", v((chunks if reduce_here else 1, blocks - 1, block, chunk), BF)),
        ("own", v((2, half, width), F32)), ("out_buf", v((8, half, width), BF)), ("in_buf", v((8, half, width), BF)),
        ("out", v((2, half, width), BF)), ("dxo", v((2, half, width), BF)),
        ("acc", v((6, 8, width), F32)), ("acc_up", v((8, hidden), F32)), ("acc_qv", v((8, 2 * local), F32)),
        ("vec", v((16, width), F32)), ("vec_out", v((5, 16, width), F32)), ("vec_in", v((5, 16, width), F32)),
        ("load_sem", dma((16,))), ("out_sem", dma((8,))), ("ex_send", dma((28,))), ("ex_recv", dma((28,))),
        ("rs_send", dma((chunks, BITS))), ("rs_recv", dma((chunks, BITS))),
    ]
    names = [n for n, *_ in inputs] + [n for n, *_ in outputs] + [n for n, *_ in scratch]
    macs = rows * width * (8 * local + 6 * hidden)
    results = pl.pallas_call(
        functools.partial(layer, reduce_here, names),
        out_shape=[o[1] for o in outputs],
        in_specs=[i[2] for i in inputs],
        out_specs=[o[2] for o in outputs],
        scratch_shapes=[s[1] for s in scratch],
        cost_estimate=pl.CostEstimate(flops=2 * macs, bytes_accessed=20 << 20, transcendentals=0),
        compiler_params=pltpu.CompilerParams(
            collective_id=0, has_side_effects=True, vmem_limit_bytes=62 << 20
        ),
    )(*[i[1] for i in inputs])
    got = dict(zip([o[0] for o in outputs], results, strict=True))
    if not reduce_here:
        n = n_dp
        grads = got["grads"].reshape(chunks, width, chunk).astype(F32)
        grads = lax.psum_scatter(grads, "dp", scatter_dimension=1, tiled=True)
        vec = lax.psum(got["vec_part"], "dp")
        at = lax.axis_index("dp")
        ups = hidden // chunk
        wide = grads.transpose(1, 0, 2)
        got["gdown"] = wide[:, :ups].reshape(width // n, hidden).T
        got["gup"] = wide[:, ups : 2 * ups].reshape(width // n, hidden)
        got["gout"] = grads[2 * ups].T
        got["gq"], got["gk"], got["gv"] = grads[2 * ups + 1], grads[2 * ups + 2], grads[2 * ups + 3]

        def mine(values):
            size = values.shape[0] // n
            return lax.dynamic_slice(values, (at * size,), (size,))

        got["g_qb"], got["g_vb"] = mine(vec[0, :local]), mine(vec[0, local:])
        got["g_ub"] = mine(vec[1:3].reshape(-1))
        for j, name in enumerate(("g_gain2", "g_shift2", "g_db", "g_gain1", "g_shift1", "g_ob")):
            got[name] = mine(vec[8 + j])
    order = (
        "os", "ol", "dxs", "dxl", "gq", "g_qb", "gk", "gv", "g_vb", "gout", "g_ob", "g_gain1", "g_shift1",
        "gup", "g_ub", "gdown", "g_db", "g_gain2", "g_shift2",
    )
    return tuple(got[n].reshape(-1) if n.startswith("g_") else got[n] for n in order)


def solution(mesh):
    in_specs = (
        P("dp", None, None), P("dp", None, None), P(None, "mp"), P("mp"), P(None, "mp"), P(None, "mp"), P("mp"),
        P("mp", None), P(), P(), P(), P(None, "mp"), P("mp"), P("mp", None), P(), P(), P(),
        P("dp", None, None), P("dp", None, None), P("dp"), P("dp"), P("dp", None),
    )
    out_specs = (
        P("dp", None, None), P("dp", None, None), P("dp", None, None), P("dp", None, None),
        P("dp", "mp"), P(("mp", "dp")), P("dp", "mp"), P("dp", "mp"), P(("mp", "dp")), P("mp", "dp"),
        P("dp"), P("dp"), P("dp"), P("dp", "mp"), P(("mp", "dp")), P("mp", "dp"), P("dp"), P("dp"), P("dp"),
    )
    return jax.shard_map(
        functools.partial(shards, mesh.shape["dp"]),
        mesh=mesh, in_specs=in_specs, out_specs=out_specs, check_vma=False,
    )
```

time: 1030 us -> 154 us (0.15)
  waiting for transfers between devices: 762 us -> 0 us
  Pallas kernels: 0 us -> 136 us
  matrix products: 93.7 us -> 0 us
  blocking collectives: 77.7 us -> 0 us
  other arithmetic: 34.8 us -> 0 us
  between operations: 19 us -> 1.42 us
  local copies, waits for them, and re-layouts: 32.3 us -> 15.9 us
    reduce_scatter x6 -> x0, waiting for transfers between devices: 696 us -> none  [the longest x1 142 us: shards(): lax.psum_scatter(downward_part, 'dp', scatter_dimension=1, tiled=True)]
    pallas_call x0 -> x1, Pallas kernels: none -> 136 us  [shards(): pl.pallas_call(functools.partial(layer, reduce_here, names), out_shape=[o...]
    dot_general x30 -> x0, matrix products: 93.7 us -> none  [the longest x1 18.5 us: shards(): jnp.dot(hidden_share_low, upward_weight, preferred_element_type=jnp.float32)]
    unnamed x1 -> x0, blocking collectives: 77.7 us -> none
    psum x4 -> x0, waiting for transfers between devices: 65.3 us -> none  [the longest x1 22.6 us: shards(): lax.psum(attn_part.astype(jnp.bfloat16), 'mp').astype(jnp.float32)]
    reduce_sum x14 -> x0, other arithmetic: 26.9 us -> none  [the longest x2 8.56 us: layer_norm(): return centred * lax.rsqrt(spread + EPSILON) * gain + shift]
  transfers between devices with their start and end apart: 10 -> 0, of which waited for: 9 -> 0; matrix products, arithmetic and copies ran while one was open for 4% -> 0% of each run, Pallas kernels for 0% -> 0%
where the time goes in v1:
time: 154 us; the launch traced here: 153 us
  Pallas kernels  136 us (88%)
  local copies, waits for them, and re-layouts  15.9 us (10%)
    pallas_call x1, Pallas kernels, shards(): pl.pallas_call(functools.partial(layer, reduce_here, names), out_shape=[o...  136 us
    unnamed x51, local copies, waits for them, and re-layouts  15.9 us

profile of v1, /device:TPU:0, one launch (start us, length us, event | category | flops | bytes accessed | tf_op | source)
XLA Modules:
  0.0 153.4 jit_solution(11966126747163922944)
XLA Ops:
  1.3 136.1 %shard_map.357 = (bf16[4,128,768]{2,1,0:T(8,128)(2,1)}, bf16[1,512,768]{2,1,0:T(8,128)(2,1)}, bf16[4,128,768]{2,1,0:T(8,128)(2,1)}, bf16[1,512,768]{2,1,0:T(8,12...) custom-call(s32[4]{0:T(128)} %refs_0_.1, ...), custom_call_target="tpu_custom_call" | custom-call | flops 19327352832 | bytes 20971520 | tf_op jit(solution)/shard_map/pallas_call | solution.py:648
  137.4 0.0 copy-start.2
  137.4 0.0 copy-start.1
  137.4 1.8 %copy.41 = f32[384,48]{0,1:T(8,128)} copy(f32[384,48]{1,0:T(8,128)} %get-tuple-element.66) | data formatting | bytes 147456
  139.2 2.1 %copy.42 = f32[1536,48]{0,1:T(8,128)} copy(f32[1536,48]{1,0:T(8,128)} %get-tuple-element.72) | data formatting | bytes 589824
  141.3 0.0 copy-start
  141.3 2.1 %copy.61 = bf16[4,128,768]{2,1,0:T(8,128)(2,1)} copy(bf16[4,128,768]{2,1,0:T(8,128)(2,1)} %get-tuple-element.95) | data formatting | bytes 1572864
  143.4 0.0 copy-done.2
  143.4 0.0 copy-start.6
  143.4 0.0 copy-start.15
  143.4 0.0 copy-start.4
  143.5 0.0 copy-start.14
  143.5 0.0 copy-start.13
  143.5 0.0 copy-start.12
  143.5 0.0 copy-start.11
  143.5 0.0 copy-start.3
  143.5 0.9 copy.62
  144.4 0.0 copy-done.1
  144.4 0.0 copy-start.7
  144.4 0.9 copy.63
  145.3 0.0 copy-done
  145.3 0.9 copy.64
  146.2 0.0 copy-done.6
  146.2 0.6 copy.65
  146.8 0.0 copy-done.15
  146.8 0.5 copy.66
  147.3 0.0 copy-done.5
  147.3 0.6 copy.67
  148.0 0.0 copy-done.4
  148.0 0.6 copy.68
  148.6 0.0 copy-done.14
  148.6 0.5 copy.69
  149.1 0.0 copy-done.13
  149.1 0.5 copy.70
  149.6 0.0 copy-done.12
  149.6 0.5 copy.71
  150.1 0.0 copy-done.11
  150.1 0.5 copy.72
  150.7 0.0 copy-done.3
  150.7 0.7 copy.73
  151.4 0.0 copy-done.10
  151.4 0.5 copy.74
  151.9 0.0 copy-done.9
  151.9 0.5 copy.75
  152.4 0.0 copy-done.8
  152.4 0.5 copy.76
  152.9 0.0 copy-done.7
  152.9 0.5 copy.77
  (4 shorter events, 0.0 us)
Async XLA Ops:
  137.4 6.0 %copy-start.2 = (bf16[1,512,768]{2,1,0:T(8,128)(2,1)S(1)}, bf16[1,512,768]{2,1,0:T(8,128)(2,1)}, u32[]{:S(2)}) copy-start(bf16[1,512,768]{2,1,0:T(8,128)(2,1)} %get-tuple-element.96) | copy-start | bytes 2359300
  137.4 7.0 %copy-start.1 = (bf16[4,128,768]{2,1,0:T(8,128)(2,1)S(1)}, bf16[4,128,768]{2,1,0:T(8,128)(2,1)}, u32[]{:S(2)}) copy-start(bf16[4,128,768]{2,1,0:T(8,128)(2,1)} %get-tuple-element.97) | copy-start | bytes 2359300
  141.3 4.0 %copy-start = (bf16[1,512,768]{2,1,0:T(8,128)(2,1)S(1)}, bf16[1,512,768]{2,1,0:T(8,128)(2,1)}, u32[]{:S(2)}) copy-start(bf16[1,512,768]{2,1,0:T(8,128)(2,1)} %get-tuple-element.98) | copy-start | bytes 2359300
  143.4 2.7 %copy-start.6 = (f32[48,384]{1,0:T(8,128)S(1)}, f32[48,384]{1,0:T(8,128)}, u32[]{:S(2)}) copy-start(f32[48,384]{1,0:T(8,128)} %get-tuple-element.99) | copy-start | bytes 221188
  143.4 3.4 %copy-start.15 = (f32[1,24]{1,0:T(1,128)S(1)}, f32[1,24]{1,0:T(1,128)}, u32[]{:S(2)}) copy-start(f32[1,24]{1,0:T(1,128)} %get-tuple-element.43) | copy-start | bytes 292
  143.4 3.9 %copy-start.5 = (f32[48,384]{1,0:T(8,128)S(1)}, f32[48,384]{1,0:T(8,128)}, u32[]{:S(2)}) copy-start(f32[48,384]{1,0:T(8,128)} %get-tuple-element.101) | copy-start | bytes 221188
  143.4 4.5 %copy-start.4 = (f32[48,384]{1,0:T(8,128)S(1)}, f32[48,384]{1,0:T(8,128)}, u32[]{:S(2)}) copy-start(f32[48,384]{1,0:T(8,128)} %get-tuple-element.102) | copy-start | bytes 221188
  143.5 5.1 %copy-start.14 = (f32[1,24]{1,0:T(1,128)S(1)}, f32[1,24]{1,0:T(1,128)}, u32[]{:S(2)}) copy-start(f32[1,24]{1,0:T(1,128)} %get-tuple-element.46) | copy-start | bytes 292
  143.5 5.6 %copy-start.13 = (f32[1,48]{1,0:T(1,128)S(1)}, f32[1,48]{1,0:T(1,128)}, u32[]{:S(2)}) copy-start(f32[1,48]{1,0:T(1,128)} %get-tuple-element.48) | copy-start | bytes 580
  143.5 6.2 %copy-start.12 = (f32[1,48]{1,0:T(1,128)S(1)}, f32[1,48]{1,0:T(1,128)}, u32[]{:S(2)}) copy-start(f32[1,48]{1,0:T(1,128)} %get-tuple-element.49) | copy-start | bytes 580
  143.5 6.7 %copy-start.11 = (f32[1,48]{1,0:T(1,128)S(1)}, f32[1,48]{1,0:T(1,128)}, u32[]{:S(2)}) copy-start(f32[1,48]{1,0:T(1,128)} %get-tuple-element.50) | copy-start | bytes 580
  143.5 7.2 %copy-start.3 = (f32[48,1536]{1,0:T(8,128)S(1)}, f32[48,1536]{1,0:T(8,128)}, u32[]{:S(2)}) copy-start(f32[48,1536]{1,0:T(8,128)} %get-tuple-element.108) | copy-start | bytes 884740
  144.4 7.0 %copy-start.10 = (f32[1,96]{1,0:T(1,128)S(1)}, f32[1,96]{1,0:T(1,128)}, u32[]{:S(2)}) copy-start(f32[1,96]{1,0:T(1,128)} %get-tuple-element.52) | copy-start | bytes 1156
  144.4 7.5 %copy-start.9 = (f32[1,48]{1,0:T(1,128)S(1)}, f32[1,48]{1,0:T(1,128)}, u32[]{:S(2)}) copy-start(f32[1,48]{1,0:T(1,128)} %get-tuple-element.54) | copy-start | bytes 580
  144.4 8.0 %copy-start.8 = (f32[1,48]{1,0:T(1,128)S(1)}, f32[1,48]{1,0:T(1,128)}, u32[]{:S(2)}) copy-start(f32[1,48]{1,0:T(1,128)} %get-tuple-element.55) | copy-start | bytes 580
  144.4 8.5 %copy-start.7 = (f32[1,48]{1,0:T(1,128)S(1)}, f32[1,48]{1,0:T(1,128)}, u32[]{:S(2)}) copy-start(f32[1,48]{1,0:T(1,128)} %get-tuple-element.56) | copy-start | bytes 580
